TPU v7x, 256 devices: a whole 4x4x8 slice. The times are simulated.
256 devices in a mesh: section: 4 (over y), row: 8 (over x, core), col: 8 (over z).
Axes of the slice: x: 4, y: 4, z: 8, core: 2. Of those that a mesh axis runs over, the one named last changes fastest.
Arguments:
- latent: bfloat16 [16, 32, 128, 256], P('section', 'row', 'col'), may hold values from -6 to 6
- w_first: bfloat16 [3, 3, 3, 256, 256], replicated, may hold values from -0.078125 to 0.078125
- w_second: bfloat16 [3, 3, 3, 256, 128], replicated, may hold values from -0.078125 to 0.078125
- w_third: bfloat16 [3, 3, 3, 128, 128], replicated, may hold values from -0.109375 to 0.109375
Outputs:
- decoded: bfloat16 [16, 64, 256, 128], P('section', 'row', 'col')
All inputs are finite; a program needn't handle non-finite values.
Results may differ from a plain program's by a relative error of at most 0.0057.
Values may be sent and summed in bfloat16 or wider, within the bound.
A program may use at most 64 MiB of HBM per device.

v0:
```python
import jax
import jax.numpy as jnp
from jax import lax
from jax.sharding import PartitionSpec as P


def shifted(x, axis, by):
    size = lax.axis_size(axis)
    pairs = [(i, i + by) for i in range(size) if 0 <= i + by < size]
    return lax.ppermute(x, axis, pairs)


def extended_2(x, sides, width):
    for axis, dim in sides:
        size, length = (lax.axis_size(axis), x.shape[dim])
        up = [(i, (i + 1) % size) for i in range(size - 1)]
        down = [(j, i) for i, j in up]
        last = lax.slice_in_dim(x, length - width, length, axis=dim)
        leading = lax.slice_in_dim(x, 0, width, axis=dim)
        before = lax.ppermute(last, axis, up)
        after = lax.ppermute(leading, axis, down)
        x = jnp.concatenate([before, x, after], axis=dim)
    return x


def upsample(field):
    frames, height, breadth, width = field.shape
    grown = jnp.broadcast_to(field[:, :, None, :, None, :], (frames, height, 2, breadth, 2, width))
    return grown.reshape(frames, 2 * height, 2 * breadth, width)


def causal_conv(padded, kernel):
    frames = padded.shape[0] - 2
    height = padded.shape[1] - 2
    breadth = padded.shape[2] - 2
    in_width = padded.shape[3]
    out_width = kernel.shape[4]
    summed = jnp.zeros((frames * height * breadth, out_width), jnp.float32)
    for row_tap in range(3):
        for col_tap in range(3):
            window = padded[:, row_tap : row_tap + height, col_tap : col_tap + breadth, :]
            stacked = jnp.concatenate(
                [window[0:frames], window[1 : frames + 1], window[2 : frames + 2]], axis=-1
            )
            tap_matrix = kernel[:, row_tap, col_tap].reshape(3 * in_width, out_width)
            summed = summed + jnp.dot(
                stacked.reshape(-1, 3 * in_width), tap_matrix, preferred_element_type=jnp.float32
            )
    return summed.reshape(frames, height, breadth, out_width)


def with_earlier(field):
    earlier = shifted(field[-2:], "section", 1)
    return jnp.concatenate([earlier, field], axis=0)


def with_fine_earlier(field):
    earlier = shifted(field[-2:], "section", 1)
    return jnp.concatenate([earlier, field], axis=0)


def per_device(latent, w_first, w_second, w_third):
    padded = extended_2(with_earlier(latent), (("row", 1), ("col", 2)), 1)
    first = causal_conv(padded, w_first).astype(jnp.bfloat16)
    extended = with_earlier(first)
    grown_inner = jnp.maximum(upsample(extended), 0)
    grown = extended_2(grown_inner, (("row", 1), ("col", 2)), 1)
    second = jnp.maximum(causal_conv(grown, w_second), 0.0).astype(jnp.bfloat16)
    second_ext = with_fine_earlier(second)
    margin_fine = extended_2(second_ext, (("row", 1), ("col", 2)), 1)
    return causal_conv(margin_fine, w_third).astype(jnp.bfloat16)


def solution(mesh):
    in_specs = (P("section", "row", "col", None), P(), P(), P())
    out_specs = P("section", "row", "col", None)
    return jax.shard_map(
        per_device, mesh=mesh, in_specs=in_specs, out_specs=out_specs, check_vma=False
    )
```

profile of v0, /device:TPU:146, one launch (start us, length us, event | category | flops | bytes accessed | tf_op | source)
XLA Modules:
  0.0 100.0 jit_solution(13498257482534083050)
XLA Ops:
  0.0 0.8 slice.501
  0.8 3.2 %collective-permute-start = (bf16[2,4,16,256]{3,2,1,0:T(8,128)(2,1)S(1)}, bf16[2,4,16,256]{3,2,1,0:T(8,128)(2,1)S(1)}, u32[]{:S(2)}, u32[]{:S(2)}) collective-permute-start(bf16[2,4,16,256]{3,2,1,0:T(8,128)(2,1)S(1)} %slice.501), channel_id=1, source_target_pairs={{0,64},{64,128},{128,192},{1,65},{65,129},{129,193},{2,66},{66,130... | collective-permute-start | bytes 196616 | tf_op jit(solution)/shard_map/ppermute | solution.py:10
  4.0 3.0 %collective-permute-done = bf16[2,4,16,256]{3,2,1,0:T(8,128)(2,1)S(1)} collective-permute-done((bf16[2,4,16,256]{3,2,1,0:T(8,128)(2,1)S(1)}, bf16[2,4,16,256]{3,2,1,0:T(8,128)(2,1)S(1)}, u32[]{:S(2)}, u32[]{:S(2)}) %collective-permute-start) | collective-permute-done | bytes 65568 | tf_op jit(solution)/shard_map/ppermute | solution.py:10
  7.0 0.9 constant_dynamic-update-slice_fusion
  7.9 1.9 %collective-permute-start.2 = (bf16[6,1,16,256]{3,2,1,0:T(8,128)(2,1)S(1)}, bf16[6,1,16,256]{3,2,1,0:T(8,128)(2,1)S(1)}, u32[]{:S(2)}, u32[]{:S(2)}) collective-permute-start(bf16[6,1,16,256]{3,2,1,0:T(8,128)(2,1)S(1)} %get-tuple-element.131), channel_id=1, source_target_pairs={{8,0},{16,8},{24,16},{32,24},{40,32},{48,40},{56,48},{9,1},{17,9},... | collective-permute-start | bytes 147464 | tf_op jit(solution)/shard_map/ppermute | solution.py:21
  9.9 2.4 %collective-permute-start.1 = (bf16[6,1,16,256]{3,2,1,0:T(8,128)(2,1)S(1)}, bf16[6,1,16,256]{3,2,1,0:T(8,128)(2,1)S(1)}, u32[]{:S(2)}, u32[]{:S(2)}) collective-permute-start(bf16[6,1,16,256]{3,2,1,0:T(8,128)(2,1)S(1)} %get-tuple-element.130), channel_id=1, source_target_pairs={{0,8},{8,16},{16,24},{24,32},{32,40},{40,48},{48,56},{1,9},{9,17},... | collective-permute-start | bytes 147464 | tf_op jit(solution)/shard_map/ppermute | solution.py:20
  12.3 2.3 %fusion.32 = (bf16[3,1,1,256,256]{4,3,2,1,0:T(8,128)(2,1)S(1)}, bf16[3,1,1,256,256]{4,3,2,1,0:T(8,128)(2,1)S(1)}, bf16[3,1,1,256,256]{4,3,2,1,0:T(8,128)(2,1)S(1...) fusion(bf16[3,3,3,256,256]{4,3,2,1,0:T(8,128)(2,1)} %param.5), kind=kLoop, calls=%fused_computation.149 | loop fusion | bytes 7077888 | tf_op jit(solution)/shard_map/slice | solution.py:45
  14.6 0.6 collective-permute-done.1
  15.3 2.0 %collective-permute-start.4 = (bf16[6,6,1,256]{3,2,1,0:T(2,128)(2,1)S(1)}, bf16[6,6,1,256]{3,2,1,0:T(2,128)(2,1)S(1)}, u32[]{:S(2)}, u32[]{:S(2)}) collective-permute-start(bf16[6,6,1,256]{3,2,1,0:T(2,128)(2,1)S(1)} %get-tuple-element.115), channel_id=1, source_target_pairs={{1,0},{2,1},{3,2},{4,3},{5,4},{6,5},{7,6},{9,8},{10,9},{11,10},{12... | collective-permute-start | bytes 55304 | tf_op jit(solution)/shard_map/ppermute | solution.py:21
  17.4 3.8 %collective-permute-start.3 = (bf16[6,6,1,256]{3,2,1,0:T(2,128)(2,1)S(1)}, bf16[6,6,1,256]{3,2,1,0:T(2,128)(2,1)S(1)}, u32[]{:S(2)}, u32[]{:S(2)}) collective-permute-start(bf16[6,6,1,256]{3,2,1,0:T(2,128)(2,1)S(1)} %get-tuple-element.116), channel_id=1, source_target_pairs={{0,1},{1,2},{2,3},{3,4},{4,5},{5,6},{6,7},{8,9},{9,10},{10,11},{11... | collective-permute-start | bytes 55304 | tf_op jit(solution)/shard_map/ppermute | solution.py:20
  21.4 3.0 %collective-permute-done.3 = bf16[6,6,1,256]{3,2,1,0:T(2,128)(2,1)S(1)} collective-permute-done((bf16[6,6,1,256]{3,2,1,0:T(2,128)(2,1)S(1)}, bf16[6,6,1,256]{3,2,1,0:T(2,128)(2,1)S(1)}, u32[]{:S(2)}, u32[]{:S(2)}) %collective-permute-start.3) | collective-permute-done | bytes 18464 | tf_op jit(solution)/shard_map/ppermute | solution.py:20
  24.7 0.3 fusion.43
  27.7 3.2 %collective-permute-start.5 = (bf16[2,4,16,256]{3,2,1,0:T(8,128)(2,1)S(1)}, bf16[2,4,16,256]{3,2,1,0:T(8,128)(2,1)S(1)}, u32[]{:S(2)}, u32[]{:S(2)}) collective-permute-start(bf16[2,4,16,256]{3,2,1,0:T(8,128)(2,1)S(1)} %bitcast.175), channel_id=1, source_target_pairs={{0,64},{64,128},{128,192},{1,65},{65,129},{129,193},{2,66},{66,130... | collective-permute-start | bytes 196616 | tf_op jit(solution)/shard_map/ppermute | solution.py:10
  30.9 1.0 %fusion.33 = (bf16[3,1,1,256,128]{4,3,2,1,0:T(8,128)(2,1)S(1)}, bf16[3,1,1,256,128]{4,3,2,1,0:T(8,128)(2,1)S(1)}, bf16[3,1,1,256,128]{4,3,2,1,0:T(8,128)(2,1)}, ...) fusion(bf16[3,3,3,256,128]{4,3,2,1,0:T(8,128)(2,1)S(1)} %copy-done), kind=kLoop, calls=%fused_computation.150 | loop fusion | bytes 3538944 | tf_op jit(solution)/shard_map/slice | solution.py:45
  31.9 1.9 %collective-permute-done.5 = bf16[2,4,16,256]{3,2,1,0:T(8,128)(2,1)S(1)} collective-permute-done((bf16[2,4,16,256]{3,2,1,0:T(8,128)(2,1)S(1)}, bf16[2,4,16,256]{3,2,1,0:T(8,128)(2,1)S(1)}, u32[]{:S(2)}, u32[]{:S(2)}) %collective-permute-start.5) | collective-permute-done | bytes 65568 | tf_op jit(solution)/shard_map/ppermute | solution.py:10
  33.9 0.7 broadcast_in_dim.12
  34.7 0.3 max.19
  35.0 0.7 fusion.38
  35.7 1.9 %collective-permute-start.6 = (bf16[6,1,32,256]{3,2,1,0:T(8,128)(2,1)}, bf16[6,1,32,256]{3,2,1,0:T(8,128)(2,1)}, u32[]{:S(2)}, u32[]{:S(2)}) collective-permute-start(bf16[6,1,32,256]{3,2,1,0:T(8,128)(2,1)} %get-tuple-element.61), channel_id=1, source_target_pairs={{0,8},{8,16},{16,24},{24,32},{32,40},{40,48},{48,56},{1,9},{9,17},... | collective-permute-start | bytes 294920 | tf_op jit(solution)/shard_map/ppermute | solution.py:20
  37.6 3.6 %collective-permute-start.7 = (bf16[6,1,32,256]{3,2,1,0:T(8,128)(2,1)}, bf16[6,1,32,256]{3,2,1,0:T(8,128)(2,1)}, u32[]{:S(2)}, u32[]{:S(2)}) collective-permute-start(bf16[6,1,32,256]{3,2,1,0:T(8,128)(2,1)} %get-tuple-element.62), channel_id=1, source_target_pairs={{8,0},{16,8},{24,16},{32,24},{40,32},{48,40},{56,48},{9,1},{17,9},... | collective-permute-start | bytes 294920 | tf_op jit(solution)/shard_map/ppermute | solution.py:21
  41.2 0.5 broadcast_in_dim.15
  41.9 0.5 broadcast_in_dim.14
  42.6 0.5 broadcast_in_dim.13
  43.4 0.9 constant_dynamic-update-slice_fusion.4
  44.6 0.9 constant_dynamic-update-slice_fusion.2
  46.0 2.6 %collective-permute-start.8 = (bf16[6,10,1,256]{3,2,1,0:T(2,128)(2,1)S(1)}, bf16[6,10,1,256]{3,2,1,0:T(2,128)(2,1)S(1)}, u32[]{:S(2)}, u32[]{:S(2)}) collective-permute-start(bf16[6,10,1,256]{3,2,1,0:T(2,128)(2,1)S(1)} %get-tuple-element.42), channel_id=1, source_target_pairs={{0,1},{1,2},{2,3},{3,4},{4,5},{5,6},{6,7},{8,9},{9,10},{10,11},{11... | collective-permute-start | bytes 92168 | tf_op jit(solution)/shard_map/ppermute | solution.py:20
  48.6 4.6 %collective-permute-start.9 = (bf16[6,10,1,256]{3,2,1,0:T(2,128)(2,1)S(1)}, bf16[6,10,1,256]{3,2,1,0:T(2,128)(2,1)S(1)}, u32[]{:S(2)}, u32[]{:S(2)}) collective-permute-start(bf16[6,10,1,256]{3,2,1,0:T(2,128)(2,1)S(1)} %get-tuple-element.41), channel_id=1, source_target_pairs={{1,0},{2,1},{3,2},{4,3},{5,4},{6,5},{7,6},{9,8},{10,9},{11,10},{12... | collective-permute-start | bytes 92168 | tf_op jit(solution)/shard_map/ppermute | solution.py:21
  53.4 0.8 copy-done.3
  54.2 0.6 fusion.49
  54.9 0.6 fusion.48
  55.5 2.7 %fusion.24 = (bf16[4,8,32,256]{3,2,1,0:T(8,128)(2,1)S(1)}, bf16[4,8,32,256]{3,2,1,0:T(8,128)(2,1)S(1)}, bf16[4,8,32,256]{3,2,1,0:T(8,128)(2,1)S(1)}, bf16[4,8,32...) fusion(bf16[6,10,32,256]{3,2,1,0:T(8,128)(2,1)S(1)} %get-tuple-, ...), kind=kLoop, calls=%fused_computation.99 | loop fusion | flops 8388608 | bytes 5208064 | tf_op jit(solution)/shard_map/concatenate | solution.py:22
  58.3 0.8 copy-done.8
  59.1 0.6 convolution_add_fusion.14
  59.7 2.7 %fusion.16 = (bf16[4,8,32,256]{3,2,1,0:T(8,128)(2,1)S(1)}, bf16[4,8,32,256]{3,2,1,0:T(8,128)(2,1)S(1)}, bf16[4,8,32,256]{3,2,1,0:T(8,128)(2,1)S(1)}, bf16[4,8,32...) fusion(bf16[6,10,32,256]{3,2,1,0:T(8,128)(2,1)S(1)} %get-tuple-, ...), kind=kLoop, calls=%fused_computation.91 | loop fusion | flops 8388608 | bytes 5208064 | tf_op jit(solution)/shard_map/concatenate | solution.py:22
  62.5 0.8 copy-done.7
  63.3 0.6 convolution_add_fusion.13
  64.0 0.8 copy-done.6
  64.8 0.6 convolution_add_fusion.12
  65.4 0.6 convolution_add_fusion.11
  66.1 0.8 copy-done.4
  66.9 0.6 convolution_add_fusion.10
  67.5 1.0 %fusion = (bf16[4,8,32,768]{3,2,1,0:T(8,128)(2,1)S(1)}, bf16[4,8,32,768]{3,2,1,0:T(8,128)(2,1)S(1)}) fusion(bf16[6,10,1,256]{3,2,1,0:T(2,128)(2,1)S(1)} %collective-permute-done.9, bf16[6,10,32,256]{3,2,1,0:T(8,128)(2,1)S(1)} %get-tuple-element.132, bf16[4,8,32,256]{3,2,1,0:T(8,128)(2,1)S(1)} %get-tuple-element.30, ...), kind=kLoop, calls=%fused_computation.17 | loop fusion | flops 12582912 | bytes 6287360 | tf_op jit(solution)/shard_map/concatenate | solution.py:42
  68.5 0.6 fusion.3
  69.1 0.6 fusion.4
  69.7 3.2 %collective-permute-start.10 = (bf16[2,8,32,128]{3,2,1,0:T(8,128)(2,1)S(1)}, bf16[2,8,32,128]{3,2,1,0:T(8,128)(2,1)S(1)}, u32[]{:S(2)}, u32[]{:S(2)}) collective-permute-start(bf16[2,8,32,128]{3,2,1,0:T(8,128)(2,1)S(1)} %bitcast.174), channel_id=1, source_target_pairs={{0,64},{64,128},{128,192},{1,65},{65,129},{129,193},{2,66},{66,130... | collective-permute-start | bytes 393224 | tf_op jit(solution)/shard_map/ppermute | solution.py:10
  73.0 4.3 %collective-permute-done.10 = bf16[2,8,32,128]{3,2,1,0:T(8,128)(2,1)S(1)} collective-permute-done((bf16[2,8,32,128]{3,2,1,0:T(8,128)(2,1)S(1)}, bf16[2,8,32,128]{3,2,1,0:T(8,128)(2,1)S(1)}, u32[]{:S(2)}, u32[]{:S(2)}) %collective-permute-start.10) | collective-permute-done | bytes 131104 | tf_op jit(solution)/shard_map/ppermute | solution.py:10
  77.3 1.9 %collective-permute-start.12 = (bf16[6,1,32,128]{3,2,1,0:T(8,128)(2,1)S(1)}, bf16[6,1,32,128]{3,2,1,0:T(8,128)(2,1)S(1)}, u32[]{:S(2)}, u32[]{:S(2)}) collective-permute-start(bf16[6,1,32,128]{3,2,1,0:T(8,128)(2,1)S(1)} %get-tuple-element.112), channel_id=1, source_target_pairs={{8,0},{16,8},{24,16},{32,24},{40,32},{48,40},{56,48},{9,1},{17,9},... | collective-permute-start | bytes 147464 | tf_op jit(solution)/shard_map/ppermute | solution.py:21
  79.2 2.4 %collective-permute-start.11 = (bf16[6,1,32,128]{3,2,1,0:T(8,128)(2,1)S(1)}, bf16[6,1,32,128]{3,2,1,0:T(8,128)(2,1)S(1)}, u32[]{:S(2)}, u32[]{:S(2)}) collective-permute-start(bf16[6,1,32,128]{3,2,1,0:T(8,128)(2,1)S(1)} %get-tuple-element.111), channel_id=1, source_target_pairs={{0,8},{8,16},{16,24},{24,32},{32,40},{40,48},{48,56},{1,9},{9,17},... | collective-permute-start | bytes 147464 | tf_op jit(solution)/shard_map/ppermute | solution.py:20
  81.8 2.8 %collective-permute-done.11 = bf16[6,1,32,128]{3,2,1,0:T(8,128)(2,1)S(1)} collective-permute-done((bf16[6,1,32,128]{3,2,1,0:T(8,128)(2,1)S(1)}, bf16[6,1,32,128]{3,2,1,0:T(8,128)(2,1)S(1)}, u32[]{:S(2)}, u32[]{:S(2)}) %collective-permute-start.11) | collective-permute-done | bytes 49184 | tf_op jit(solution)/shard_map/ppermute | solution.py:20
  84.7 2.2 %collective-permute-start.14 = (bf16[6,10,1,128]{3,2,1,0:T(2,128)(2,1)S(1)}, bf16[6,10,1,128]{3,2,1,0:T(2,128)(2,1)S(1)}, u32[]{:S(2)}, u32[]{:S(2)}) collective-permute-start(bf16[6,10,1,128]{3,2,1,0:T(2,128)(2,1)S(1)} %get-tuple-element.83), channel_id=1, source_target_pairs={{1,0},{2,1},{3,2},{4,3},{5,4},{6,5},{7,6},{9,8},{10,9},{11,10},{12... | collective-permute-start | bytes 46088 | tf_op jit(solution)/shard_map/ppermute | solution.py:21
  86.9 3.9 %collective-permute-start.13 = (bf16[6,10,1,128]{3,2,1,0:T(2,128)(2,1)S(1)}, bf16[6,10,1,128]{3,2,1,0:T(2,128)(2,1)S(1)}, u32[]{:S(2)}, u32[]{:S(2)}) collective-permute-start(bf16[6,10,1,128]{3,2,1,0:T(2,128)(2,1)S(1)} %get-tuple-element.84), channel_id=1, source_target_pairs={{0,1},{1,2},{2,3},{3,4},{4,5},{5,6},{6,7},{8,9},{9,10},{10,11},{11... | collective-permute-start | bytes 46088 | tf_op jit(solution)/shard_map/ppermute | solution.py:20
  91.3 2.5 %collective-permute-done.13 = bf16[6,10,1,128]{3,2,1,0:T(2,128)(2,1)S(1)} collective-permute-done((bf16[6,10,1,128]{3,2,1,0:T(2,128)(2,1)S(1)}, bf16[6,10,1,128]{3,2,1,0:T(2,128)(2,1)S(1)}, u32[]{:S(2)}, u32[]{:S(2)}) %collective-permute-start.13) | collective-permute-done | bytes 15392 | tf_op jit(solution)/shard_map/ppermute | solution.py:20
  93.9 0.4 pad_maximum_fusion.18
  94.3 0.4 fusion.40
  94.7 0.5 fusion.39
  95.3 0.4 fusion.50
  95.7 0.4 convolution_add_fusion.7
  96.2 0.4 convolution_add_fusion.6
  96.7 0.4 convolution_add_fusion.5
  97.1 0.4 convolution_add_fusion.4
  97.6 0.4 convolution_add_fusion.3
  98.1 0.4 convolution_add_fusion.2
  98.4 0.4 convolution_add_fusion.1
  98.9 1.1 %fusion.5 = bf16[1024,128]{1,0:T(8,128)(2,1)} fusion(f32[1024,128]{1,0:T(8,128)S(1)} %convolution_add_fusion.1, bf16[1024,384]{1,0:T(8,128)(2,1)S(1)} %bitcast.128, bf16[384,128]{1,0:T(8,128)(2,1)S(1)} %bitcast.165), kind=kOutput, calls=%fused_computation.45 | convolution fusion | flops 100925440 | bytes 1671168 | tf_op jit(solution)/shard_map/dot_general | solution.py:46
  (76 shorter events, 6.7 us)
Async XLA Ops:
  0.8 6.1 %collective-permute-start = (bf16[2,4,16,256]{3,2,1,0:T(8,128)(2,1)S(1)}, bf16[2,4,16,256]{3,2,1,0:T(8,128)(2,1)S(1)}, u32[]{:S(2)}, u32[]{:S(2)}) collective-permute-start(bf16[2,4,16,256]{3,2,1,0:T(8,128)(2,1)S(1)} %slice.501), channel_id=1, source_target_pairs={{0,64},{64,128},{128,192},{1,65},{65,129},{129,193},{2,66},{66,130... | collective-permute-start | bytes 196616 | tf_op jit(solution)/shard_map/ppermute | solution.py:10
  7.9 6.7 %collective-permute-start.2 = (bf16[6,1,16,256]{3,2,1,0:T(8,128)(2,1)S(1)}, bf16[6,1,16,256]{3,2,1,0:T(8,128)(2,1)S(1)}, u32[]{:S(2)}, u32[]{:S(2)}) collective-permute-start(bf16[6,1,16,256]{3,2,1,0:T(8,128)(2,1)S(1)} %get-tuple-element.131), channel_id=1, source_target_pairs={{8,0},{16,8},{24,16},{32,24},{40,32},{48,40},{56,48},{9,1},{17,9},... | collective-permute-start | bytes 147464 | tf_op jit(solution)/shard_map/ppermute | solution.py:21
  9.9 5.4 %collective-permute-start.1 = (bf16[6,1,16,256]{3,2,1,0:T(8,128)(2,1)S(1)}, bf16[6,1,16,256]{3,2,1,0:T(8,128)(2,1)S(1)}, u32[]{:S(2)}, u32[]{:S(2)}) collective-permute-start(bf16[6,1,16,256]{3,2,1,0:T(8,128)(2,1)S(1)} %get-tuple-element.130), channel_id=1, source_target_pairs={{0,8},{8,16},{16,24},{24,32},{32,40},{40,48},{48,56},{1,9},{9,17},... | collective-permute-start | bytes 147464 | tf_op jit(solution)/shard_map/ppermute | solution.py:20
  14.6 6.6 %copy-start.2 = (bf16[4,4,16,256]{3,2,1,0:T(8,128)(2,1)S(1)}, bf16[4,4,16,256]{3,2,1,0:T(8,128)(2,1)}, u32[]{:S(2)}) copy-start(bf16[4,4,16,256]{3,2,1,0:T(8,128)(2,1)} %param.4) | copy-start | bytes 393220
  15.3 6.0 %collective-permute-start.4 = (bf16[6,6,1,256]{3,2,1,0:T(2,128)(2,1)S(1)}, bf16[6,6,1,256]{3,2,1,0:T(2,128)(2,1)S(1)}, u32[]{:S(2)}, u32[]{:S(2)}) collective-permute-start(bf16[6,6,1,256]{3,2,1,0:T(2,128)(2,1)S(1)} %get-tuple-element.115), channel_id=1, source_target_pairs={{1,0},{2,1},{3,2},{4,3},{5,4},{6,5},{7,6},{9,8},{10,9},{11,10},{12... | collective-permute-start | bytes 55304 | tf_op jit(solution)/shard_map/ppermute | solution.py:21
  17.4 7.1 %collective-permute-start.3 = (bf16[6,6,1,256]{3,2,1,0:T(2,128)(2,1)S(1)}, bf16[6,6,1,256]{3,2,1,0:T(2,128)(2,1)S(1)}, u32[]{:S(2)}, u32[]{:S(2)}) collective-permute-start(bf16[6,6,1,256]{3,2,1,0:T(2,128)(2,1)S(1)} %get-tuple-element.116), channel_id=1, source_target_pairs={{0,1},{1,2},{2,3},{3,4},{4,5},{5,6},{6,7},{8,9},{9,10},{10,11},{11... | collective-permute-start | bytes 55304 | tf_op jit(solution)/shard_map/ppermute | solution.py:20
  27.1 3.8 %copy-start = (bf16[3,3,3,256,128]{4,3,2,1,0:T(8,128)(2,1)S(1)}, bf16[3,3,3,256,128]{4,3,2,1,0:T(8,128)(2,1)}, u32[]{:S(2)}) copy-start(bf16[3,3,3,256,128]{4,3,2,1,0:T(8,128)(2,1)} %param.6) | copy-start | bytes 5308420
  27.7 6.2 %collective-permute-start.5 = (bf16[2,4,16,256]{3,2,1,0:T(8,128)(2,1)S(1)}, bf16[2,4,16,256]{3,2,1,0:T(8,128)(2,1)S(1)}, u32[]{:S(2)}, u32[]{:S(2)}) collective-permute-start(bf16[2,4,16,256]{3,2,1,0:T(8,128)(2,1)S(1)} %bitcast.175), channel_id=1, source_target_pairs={{0,64},{64,128},{128,192},{1,65},{65,129},{129,193},{2,66},{66,130... | collective-permute-start | bytes 196616 | tf_op jit(solution)/shard_map/ppermute | solution.py:10
  35.7 7.8 %collective-permute-start.6 = (bf16[6,1,32,256]{3,2,1,0:T(8,128)(2,1)}, bf16[6,1,32,256]{3,2,1,0:T(8,128)(2,1)}, u32[]{:S(2)}, u32[]{:S(2)}) collective-permute-start(bf16[6,1,32,256]{3,2,1,0:T(8,128)(2,1)} %get-tuple-element.61), channel_id=1, source_target_pairs={{0,8},{8,16},{16,24},{24,32},{32,40},{40,48},{48,56},{1,9},{9,17},... | collective-permute-start | bytes 294920 | tf_op jit(solution)/shard_map/ppermute | solution.py:20
  37.6 7.0 %collective-permute-start.7 = (bf16[6,1,32,256]{3,2,1,0:T(8,128)(2,1)}, bf16[6,1,32,256]{3,2,1,0:T(8,128)(2,1)}, u32[]{:S(2)}, u32[]{:S(2)}) collective-permute-start(bf16[6,1,32,256]{3,2,1,0:T(8,128)(2,1)} %get-tuple-element.62), channel_id=1, source_target_pairs={{8,0},{16,8},{24,16},{32,24},{40,32},{48,40},{56,48},{9,1},{17,9},... | collective-permute-start | bytes 294920 | tf_op jit(solution)/shard_map/ppermute | solution.py:21
  46.0 9.5 %collective-permute-start.8 = (bf16[6,10,1,256]{3,2,1,0:T(2,128)(2,1)S(1)}, bf16[6,10,1,256]{3,2,1,0:T(2,128)(2,1)S(1)}, u32[]{:S(2)}, u32[]{:S(2)}) collective-permute-start(bf16[6,10,1,256]{3,2,1,0:T(2,128)(2,1)S(1)} %get-tuple-element.42), channel_id=1, source_target_pairs={{0,1},{1,2},{2,3},{3,4},{4,5},{5,6},{6,7},{8,9},{9,10},{10,11},{11... | collective-permute-start | bytes 92168 | tf_op jit(solution)/shard_map/ppermute | solution.py:20
  48.6 11.0 %collective-permute-start.9 = (bf16[6,10,1,256]{3,2,1,0:T(2,128)(2,1)S(1)}, bf16[6,10,1,256]{3,2,1,0:T(2,128)(2,1)S(1)}, u32[]{:S(2)}, u32[]{:S(2)}) collective-permute-start(bf16[6,10,1,256]{3,2,1,0:T(2,128)(2,1)S(1)} %get-tuple-element.41), channel_id=1, source_target_pairs={{1,0},{2,1},{3,2},{4,3},{5,4},{6,5},{7,6},{9,8},{10,9},{11,10},{12... | collective-permute-start | bytes 92168 | tf_op jit(solution)/shard_map/ppermute | solution.py:21
  53.3 0.9 copy-start.3
  58.1 0.9 copy-start.8
  62.4 0.9 copy-start.7
  63.9 0.9 copy-start.6
  64.0 1.4 %copy-start.5 = (bf16[3,1,1,256,128]{4,3,2,1,0:T(8,128)(2,1)S(1)}, bf16[3,1,1,256,128]{4,3,2,1,0:T(8,128)(2,1)}, u32[]{:S(2)}) copy-start(bf16[3,1,1,256,128]{4,3,2,1,0:T(8,128)(2,1)} %get-tuple-element.17) | copy-start | bytes 589828
  66.0 0.9 copy-start.4
  69.1 3.8 %copy-start.1 = (bf16[3,3,3,128,128]{4,3,2,1,0:T(8,128)(2,1)S(1)}, bf16[3,3,3,128,128]{4,3,2,1,0:T(8,128)(2,1)}, u32[]{:S(2)}) copy-start(bf16[3,3,3,128,128]{4,3,2,1,0:T(8,128)(2,1)} %param.7) | copy-start | bytes 2654212
  69.7 7.6 %collective-permute-start.10 = (bf16[2,8,32,128]{3,2,1,0:T(8,128)(2,1)S(1)}, bf16[2,8,32,128]{3,2,1,0:T(8,128)(2,1)S(1)}, u32[]{:S(2)}, u32[]{:S(2)}) collective-permute-start(bf16[2,8,32,128]{3,2,1,0:T(8,128)(2,1)S(1)} %bitcast.174), channel_id=1, source_target_pairs={{0,64},{64,128},{128,192},{1,65},{65,129},{129,193},{2,66},{66,130... | collective-permute-start | bytes 393224 | tf_op jit(solution)/shard_map/ppermute | solution.py:10
  77.3 4.5 %collective-permute-start.12 = (bf16[6,1,32,128]{3,2,1,0:T(8,128)(2,1)S(1)}, bf16[6,1,32,128]{3,2,1,0:T(8,128)(2,1)S(1)}, u32[]{:S(2)}, u32[]{:S(2)}) collective-permute-start(bf16[6,1,32,128]{3,2,1,0:T(8,128)(2,1)S(1)} %get-tuple-element.112), channel_id=1, source_target_pairs={{8,0},{16,8},{24,16},{32,24},{40,32},{48,40},{56,48},{9,1},{17,9},... | collective-permute-start | bytes 147464 | tf_op jit(solution)/shard_map/ppermute | solution.py:21
  79.2 5.4 %collective-permute-start.11 = (bf16[6,1,32,128]{3,2,1,0:T(8,128)(2,1)S(1)}, bf16[6,1,32,128]{3,2,1,0:T(8,128)(2,1)S(1)}, u32[]{:S(2)}, u32[]{:S(2)}) collective-permute-start(bf16[6,1,32,128]{3,2,1,0:T(8,128)(2,1)S(1)} %get-tuple-element.111), channel_id=1, source_target_pairs={{0,8},{8,16},{16,24},{24,32},{32,40},{40,48},{48,56},{1,9},{9,17},... | collective-permute-start | bytes 147464 | tf_op jit(solution)/shard_map/ppermute | solution.py:20
  84.7 6.7 %collective-permute-start.14 = (bf16[6,10,1,128]{3,2,1,0:T(2,128)(2,1)S(1)}, bf16[6,10,1,128]{3,2,1,0:T(2,128)(2,1)S(1)}, u32[]{:S(2)}, u32[]{:S(2)}) collective-permute-start(bf16[6,10,1,128]{3,2,1,0:T(2,128)(2,1)S(1)} %get-tuple-element.83), channel_id=1, source_target_pairs={{1,0},{2,1},{3,2},{4,3},{5,4},{6,5},{7,6},{9,8},{10,9},{11,10},{12... | collective-permute-start | bytes 46088 | tf_op jit(solution)/shard_map/ppermute | solution.py:21
  86.9 7.0 %collective-permute-start.13 = (bf16[6,10,1,128]{3,2,1,0:T(2,128)(2,1)S(1)}, bf16[6,10,1,128]{3,2,1,0:T(2,128)(2,1)S(1)}, u32[]{:S(2)}, u32[]{:S(2)}) collective-permute-start(bf16[6,10,1,128]{3,2,1,0:T(2,128)(2,1)S(1)} %get-tuple-element.84), channel_id=1, source_target_pairs={{0,1},{1,2},{2,3},{3,4},{4,5},{5,6},{6,7},{8,9},{9,10},{10,11},{11... | collective-permute-start | bytes 46088 | tf_op jit(solution)/shard_map/ppermute | solution.py:20
where the time goes:
time: 101 us; the launch traced here: 100 us
  starting transfers between devices  42.9 us (42%)
  waiting for transfers between devices  18.3 us (18%)
  local copies, waits for them, and re-layouts  17 us (17%)
  matrix products  11.6 us (11%)
  other arithmetic  9.34 us (9%)
    ppermute x6, starting transfers between devices, extended_2(): before = lax.ppermute(last, axis, up)  17 us
    ppermute x6, starting transfers between devices, extended_2(): after = lax.ppermute(leading, axis, down)  16.3 us
    dot_general x27, matrix products, causal_conv(): jnp.dot(stacked.reshape(-1, 3 * in_width), tap_matrix, preferred_element_...  11.6 us
    ppermute x3, starting transfers between devices, shifted(): return lax.ppermute(x, axis, pairs)  9.56 us
    ppermute x3, waiting for transfers between devices, shifted(): return lax.ppermute(x, axis, pairs)  9.19 us
    ppermute x6, waiting for transfers between devices, extended_2(): before = lax.ppermute(last, axis, up)  9.06 us
    concatenate x8, other arithmetic, extended_2(): x = jnp.concatenate([before, x, after], axis=dim)  6.28 us
    unnamed x21, local copies, waits for them, and re-layouts  5.19 us
  transfers between devices with their start and end apart: 15, of which 7 were waited for; matrix products, arithmetic and copies ran while one was open for 12% of the time, Pallas kernels for 0%

commit v1 on v0

v1 whole, which is shorter than its diff:
```python
import functools

import jax
import jax.numpy as jnp
import numpy as np
from jax import lax
from jax.experimental import pallas as pl
from jax.experimental.pallas import tpu as pltpu
from jax.sharding import PartitionSpec as P

MESH = pl.DeviceIdType.MESH
BF16 = jnp.bfloat16
F32 = jnp.float32

T, R, C = 4, 4, 16
LAT, MID = 256, 128
DIRS = [(dr, dc) for dr in (-1, 0, 1) for dc in (-1, 0, 1) if (dr, dc) != (0, 0)]
GROUPS = {"A": (3, 5), "B1": (2, 3), "B0": (1, 2), "C": (0, 1)}
ORDER = {"A": 0, "B1": 1, "B0": 2, "C": 3}
TAPS = [(dr, dc) for dr in range(3) for dc in range(3)]


def selections():
    sel = np.zeros((2, 400, 224), np.float32)

    def source(t2, row, col):
        if 2 <= col < 18:
            return row * C + col - 2
        side = 0 if col < 2 else 1
        slot, r = (0, row + 2) if row < 2 else (1, row - 2) if row < 6 else (2, row - 6)
        base = 128 if side == 1 else 176
        return base + slot * 16 + r * 4 + t2 * 2 + (col if side == 0 else col - 18)

    for t2 in range(2):
        for row in range(8):
            for j in range(C):
                sel[t2, row * C + j, source(t2, row, j)] = 1
                sel[t2, 128 + row * C + j, source(t2, row, j + 1)] = 1
        for tap, (dr, dc) in enumerate(TAPS):
            for j in range(2):
                for r in range(6):
                    sel[t2, 256 + tap * 16 + j * 8 + r, source(t2, r + dr, 16 + j + dc)] = 1
    pack = np.zeros((32, 128), np.float32)
    for side in range(2):
        for r in range(R):
            for t2 in range(2):
                for c in range(2):
                    pack[side * 16 + r * 4 + t2 * 2 + c, t2 * 64 + r * C + c + 14 * side] = 1
    return sel.astype(jnp.bfloat16), pack.astype(jnp.bfloat16)


def kernel(
    sizes, latent, w1_hbm, w2_hbm, w3_hbm, sel_ref, pack_ref, out_ref,
    rc, halo, pack, m0, m1, e9, f0, f1, e2, s0, s1, w1, w2, w2e, w3e,
    send, recv, ysend, yrecv, local,
):
    sections, rows, cols = sizes
    s, r, c = (lax.axis_index(a) for a in ("section", "row", "col"))

    def device(ds, dr, dc):
        return (
            lax.rem(s + ds + sections, sections),
            lax.rem(r + dr + rows, rows),
            lax.rem(c + dc + cols, cols),
        )

    def inside(i, size):
        return jnp.logical_and(i >= 0, i < size)

    def spatial(group, k):
        dr, dc = DIRS[k]
        g0, g1 = GROUPS[group]
        n = ORDER[group]
        if dc == 0:
            src = rc.at[2 * g0 : 2 * g1, pl.ds(4 if dr == 1 else 2, 2)]
            dst = rc.at[2 * g0 : 2 * g1, pl.ds(0 if dr == 1 else 6, 2)]
        else:
            side = 1 if dc == 1 else 0
            src = pack.at[side, g0:g1]
            dst = halo.at[1 - side, 1 - dr, g0:g1]
        return pltpu.make_async_remote_copy(
            src_ref=src, dst_ref=dst, send_sem=send.at[n, k], recv_sem=recv.at[n, k],
            device_id=device(0, dr, dc), device_id_type=MESH,
        )

    def sends(k):
        dr, dc = DIRS[k]
        return jnp.logical_and(inside(r + dr, rows), inside(c + dc, cols))

    def receives(k):
        dr, dc = DIRS[k]
        return jnp.logical_and(inside(r - dr, rows), inside(c - dc, cols))

    def spatial_start(group):
        for k in range(8):
            @pl.when(sends(k))
            def _():
                spatial(group, k).start()

    def spatial_wait_recv(group):
        for k in range(8):
            @pl.when(receives(k))
            def _():
                spatial(group, k).wait_recv()

    def spatial_wait_send(group):
        for k in range(8):
            @pl.when(sends(k))
            def _():
                spatial(group, k).wait_send()

    def onward(n):
        src, dst = ((8, 4), (6, 2), (4, 0))[n]
        return pltpu.make_async_remote_copy(
            src_ref=rc.at[pl.ds(src, 2), 2:6], dst_ref=rc.at[pl.ds(dst, 2), 2:6],
            send_sem=ysend.at[n], recv_sem=yrecv.at[n],
            device_id=device(1, 0, 0), device_id_type=MESH,
        )

    def make_pack(g):
        own = rc[2 * g : 2 * g + 2, 2:6].reshape(2 * R * C, LAT)
        both = jnp.dot(pack_ref[...], own, preferred_element_type=F32).astype(BF16)
        pack[0, g] = both[0:16]
        pack[1, g] = both[16:32]

    tile = pltpu.make_async_copy(latent, rc.at[6:10, 2:6], local.at[0])
    tile.start()
    second_copy = pltpu.make_async_copy(w2_hbm, w2, local.at[1])
    second_copy.start()
    first_copy = pltpu.make_async_copy(w1_hbm, w1, local.at[2])
    first_copy.start()
    third_copies = []
    for n, (e, p, fi, fo) in enumerate(
        [(0, 0, 0, 0), (1, 0, 1, 0), (0, 0, 1, 1), (2, 1, 0, 0), (1, 1, 0, 1), (2, 1, 1, 1)]
    ):
        copy = pltpu.make_async_copy(
            w3_hbm.at[:, :, e],
            w3e.at[:, p, :, fi * MID : (fi + 1) * MID, fo * MID : (fo + 1) * MID],
            local.at[3 + n],
        )
        copy.start()
        third_copies.append(copy)

    barrier = pltpu.get_barrier_semaphore()
    partners = [(0, dr, dc) for dr, dc in DIRS] + [(1, 0, 0), (-1, 0, 0)]
    for d in partners:
        pl.semaphore_signal(barrier, inc=1, device_id=device(*d), device_id_type=MESH)

    tile.wait()
    make_pack(4)
    make_pack(3)
    pl.semaphore_wait(barrier, len(partners))

    @pl.when(s < sections - 1)
    def _():
        onward(0).start()

    spatial_start("A")

    @pl.when(s < sections - 1)
    def _():
        onward(1).start()

    @pl.when(r == 0)
    def _():
        rc[:, 0:2] = jnp.zeros((10, 2, C, LAT), BF16)
        halo[:, 0] = jnp.zeros((2, 5, 16, LAT), BF16)

    @pl.when(r == rows - 1)
    def _():
        rc[:, 6:8] = jnp.zeros((10, 2, C, LAT), BF16)
        halo[:, 2] = jnp.zeros((2, 5, 16, LAT), BF16)

    @pl.when(c == 0)
    def _():
        halo[0] = jnp.zeros((3, 5, 16, LAT), BF16)

    @pl.when(c == cols - 1)
    def _():
        halo[1] = jnp.zeros((3, 5, 16, LAT), BF16)

    @pl.when(s == 0)
    def _():
        rc[2:6] = jnp.zeros((4, 8, C, LAT), BF16)
        halo[:, :, 1:3] = jnp.zeros((2, 3, 2, 16, LAT), BF16)

    @pl.when(s <= 1)
    def _():
        rc[0:2] = jnp.zeros((2, 8, C, LAT), BF16)
        halo[:, :, 0:1] = jnp.zeros((2, 3, 1, 16, LAT), BF16)

    w3e[:, 0, :, 0:MID, MID:] = jnp.zeros((3, 3, MID, MID), BF16)
    w3e[:, 1, :, MID:, 0:MID] = jnp.zeros((3, 3, MID, MID), BF16)

    second_copy.wait()
    pick = {(0, 0): (0, 1), (0, 1): (2,), (1, 0): (0,), (1, 1): (1, 2)}

    @pl.loop(0, 3)
    def _(a):
        for fr in range(2):
            for q in range(2):
                column = []
                for e in range(3):
                    x = [w2[a, b, e].astype(F32) for b in pick[fr, q]]
                    column.append(functools.reduce(jnp.add, x))
                for fc in range(2):
                    for p in range(2):
                        x = functools.reduce(jnp.add, [column[e] for e in pick[fc, p]])
                        lane = (fr * 2 + fc) * MID
                        row = (q * 2 + p) * LAT
                        w2e[a, row : row + LAT, lane : lane + MID] = x.astype(BF16)

    def prepare(t):
        g, t2 = t // 2, t % 2
        rhs = jnp.concatenate(
            [rc[t].reshape(8 * C, LAT), halo[1, :, g].reshape(48, LAT), halo[0, :, g].reshape(48, LAT)],
            axis=0,
        )
        moved = jnp.dot(sel_ref[t2], rhs, preferred_element_type=F32).astype(BF16)
        m0[t] = moved[0:128].reshape(8, C, LAT)
        m1[t] = moved[128:256].reshape(8, C, LAT)
        for tap in range(9):
            e9[t, :, tap * LAT : (tap + 1) * LAT] = moved[256 + tap * 16 : 272 + tap * 16]

    row16 = lax.broadcasted_iota(jnp.int32, (16, 1), 0)
    top, bottom = r == 0, r == rows - 1
    leftmost, rightmost = c == 0, c == cols - 1

    def shifted_up(x, last):
        return jnp.where(row16 == 15, last, pltpu.roll(x, 15, 0))

    def conv1(f):
        shifts = (m0, m1, rc)
        blocks = []
        for a in range(3):
            for tap, (dr, dc) in enumerate(TAPS):
                x = shifts[dc]
                blocks.append(
                    jnp.concatenate(
                        [x[f + a, dr : dr + 6].reshape(96, LAT), x[f + 1 + a, dr : dr + 6].reshape(96, LAT),
                         e9[f + a, :, tap * LAT : (tap + 1) * LAT], e9[f + 1 + a, :, tap * LAT : (tap + 1) * LAT]],
                        axis=0,
                    )
                )
        lhs = jnp.concatenate(blocks, axis=1)
        total = jnp.dot(lhs, w1[...].reshape(27 * LAT, LAT), preferred_element_type=F32)
        total = jnp.maximum(total, 0.0)
        for i in range(2):
            main = total[i * 96 : i * 96 + 96].reshape(6, 16, LAT)
            edge = total[192 + i * 16 : 208 + i * 16]
            row8 = row16 % 8
            bad = jnp.logical_or(
                jnp.logical_or(jnp.logical_and(row8 == 0, top), jnp.logical_and(row8 == 5, bottom)),
                jnp.logical_and(row16 >= 8, rightmost),
            )
            edge = jnp.where(jnp.logical_or(bad, row8 >= 6), 0.0, edge)
            for q in range(6):
                bad = jnp.logical_and(row16 == 0, leftmost)
                if q == 0:
                    bad = jnp.logical_or(bad, top)
                if q == 5:
                    bad = jnp.logical_or(bad, bottom)
                x = jnp.where(bad, 0.0, main[q])
                f0[f + i, q] = x.astype(BF16)
                f1[f + i, q] = shifted_up(x, edge[q : q + 1]).astype(BF16)
            nothing = jnp.zeros((8, LAT), F32)
            for p in range(2):
                x = edge[p * 8 : p * 8 + 8]
                for q, y in ((0, x), (1, pltpu.roll(x, 7, 0))):
                    lane = (q * 2 + p) * LAT
                    e2[f + i, :, lane : lane + LAT] = jnp.concatenate([y, nothing], axis=0).astype(BF16)

    def conv2(f):
        shifts = (f0, f1)
        blocks = []
        for a in range(3):
            for q in range(2):
                for p in range(2):
                    x = shifts[p]
                    lane = (q * 2 + p) * LAT
                    blocks.append(
                        jnp.concatenate(
                            [x[f + a, q : q + 5].reshape(80, LAT), x[f + 1 + a, q : q + 5].reshape(80, LAT),
                             e2[f + a, :, lane : lane + LAT], e2[f + 1 + a, :, lane : lane + LAT]],
                            axis=0,
                        )
                    )
        lhs = jnp.concatenate(blocks, axis=1)
        total = jnp.dot(lhs, w2e[...].reshape(12 * LAT, 4 * MID), preferred_element_type=F32)
        total = jnp.maximum(total, 0.0)
        for i in range(2):
            for lane in range(4):
                fr, fc = lane // 2, lane % 2
                cut = slice(lane * MID, (lane + 1) * MID)
                edge = total[160 + i * 16 : 176 + i * 16, cut]
                bad = jnp.logical_and(row16 == (0 if fr == 0 else 4), top if fr == 0 else bottom)
                if fc == 1:
                    bad = jnp.logical_or(bad, rightmost)
                edge = jnp.where(bad, 0.0, edge)
                for q in range(5):
                    x = total[i * 80 + q * 16 : i * 80 + q * 16 + 16, cut]
                    if fc == 0:
                        x = jnp.where(jnp.logical_and(row16 == 0, leftmost), 0.0, x)
                    if fr == 0 and q == 0:
                        x = jnp.where(top, 0.0, x)
                    if fr == 1 and q == 4:
                        x = jnp.where(bottom, 0.0, x)
                    s0[f + i, q, :, cut] = x.astype(BF16)
                    s1[f + i, q, :, cut] = shifted_up(x, edge[q : q + 1]).astype(BF16)

    def conv3(f):
        shifts = (s0, s1)
        blocks = []
        for a in range(3):
            for p in range(2):
                for b in range(3):
                    parts = []
                    for parity in range(2):
                        q, fr = divmod(b + parity, 2)
                        for i in range(2):
                            x = shifts[p][f + i + a, q : q + 4, :, fr * 256 : fr * 256 + 256]
                            parts.append(x.reshape(64, 256))
                    blocks.append(jnp.concatenate(parts, axis=0))
        lhs = jnp.concatenate(blocks, axis=1)
        total = jnp.dot(lhs, w3e[...].reshape(18 * 256, 256), preferred_element_type=F32).astype(BF16)
        for parity in range(2):
            for i in range(2):
                for q in range(4):
                    at = parity * 128 + i * 64 + q * 16
                    out_ref[f + i, 2 * q + parity] = total[at : at + 16]

    spatial_wait_recv("A")
    for t in (8, 9, 6, 7):
        prepare(t)

    @pl.when(s > 0)
    def _():
        onward(0).wait_recv()

        @pl.when(s < sections - 1)
        def _():
            onward(2).start()

        make_pack(2)
        spatial_start("B1")

    first_copy.wait()
    conv1(6)

    @pl.when(s > 0)
    def _():
        onward(1).wait_recv()
        make_pack(1)
        spatial_start("B0")
        spatial_wait_recv("B1")

    prepare(4)
    prepare(5)
    conv1(4)
    conv2(4)

    @pl.when(s > 1)
    def _():
        onward(2).wait_recv()
        make_pack(0)
        spatial_start("C")

    @pl.when(s > 0)
    def _():
        spatial_wait_recv("B0")

    prepare(2)
    prepare(3)
    conv1(2)
    conv2(2)
    for copy in third_copies:
        copy.wait()
    conv3(2)

    @pl.when(s > 1)
    def _():
        spatial_wait_recv("C")

    prepare(0)
    prepare(1)
    conv1(0)
    conv2(0)
    conv3(0)

    spatial_wait_send("A")

    @pl.when(s < sections - 1)
    def _():
        onward(0).wait_send()
        onward(1).wait_send()

    @pl.when(s > 0)
    def _():
        spatial_wait_send("B1")
        spatial_wait_send("B0")

        @pl.when(s < sections - 1)
        def _():
            onward(2).wait_send()

    @pl.when(s > 1)
    def _():
        spatial_wait_send("C")


def solution(mesh):
    sizes = tuple(mesh.shape[a] for a in ("section", "row", "col"))
    sel, pack = selections()

    def per_device(latent, w_first, w_second, w_third):
        hbm = pl.BlockSpec(memory_space=pltpu.HBM)
        vmem = pl.BlockSpec(memory_space=pltpu.VMEM)
        out = pl.pallas_call(
            functools.partial(kernel, sizes),
            out_shape=jax.ShapeDtypeStruct((T, 2 * R, C, 2 * MID), BF16),
            in_specs=[hbm] * 4 + [vmem] * 2,
            out_specs=vmem,
            scratch_shapes=[
                pltpu.VMEM((10, 8, C, LAT), BF16),
                pltpu.VMEM((2, 3, 5, 16, LAT), BF16),
                pltpu.VMEM((2, 5, 16, LAT), BF16),
                pltpu.VMEM((10, 8, C, LAT), BF16),
                pltpu.VMEM((10, 8, C, LAT), BF16),
                pltpu.VMEM((10, 16, 9 * LAT), BF16),
                pltpu.VMEM((8, 6, 16, LAT), BF16),
                pltpu.VMEM((8, 6, 16, LAT), BF16),
                pltpu.VMEM((8, 16, 4 * LAT), BF16),
                pltpu.VMEM((6, 5, 16, 4 * MID), BF16),
                pltpu.VMEM((6, 5, 16, 4 * MID), BF16),
                pltpu.VMEM((3, 3, 3, LAT, LAT), BF16),
                pltpu.VMEM((3, 3, 3, LAT, MID), BF16),
                pltpu.VMEM((3, 4 * LAT, 4 * MID), BF16),
                pltpu.VMEM((3, 2, 3, 2 * MID, 2 * MID), BF16),
                pltpu.SemaphoreType.DMA((4, 8)),
                pltpu.SemaphoreType.DMA((4, 8)),
                pltpu.SemaphoreType.DMA((3,)),
                pltpu.SemaphoreType.DMA((3,)),
                pltpu.SemaphoreType.DMA((9,)),
            ],
            compiler_params=pltpu.CompilerParams(
                collective_id=0, has_side_effects=True, vmem_limit_bytes=56 * 1024 * 1024
            ),
            cost_estimate=pl.CostEstimate(flops=7 * 10**9, bytes_accessed=8 * 10**6, transcendentals=0),
            name="decoder_block",
        )(latent, w_first, w_second, w_third, jnp.asarray(sel), jnp.asarray(pack))
        return out.reshape(T, 2 * R, 2 * C, MID)

    spec = P("section", "row", "col", None)
    return jax.shard_map(
        per_device, mesh=mesh, in_specs=(spec, P(), P(), P()), out_specs=spec, check_vma=False
    )
```

time: 101 us -> 30.4 us (0.30)
  the two profiles are of different devices: /device:TPU:146 before, /device:TPU:27 now
where the time goes in v1:
time: 30.4 us; the launch traced here: 30.1 us
  Pallas kernels  28.4 us (93%)
  local copies, waits for them, and re-layouts  1.74 us (6%)
    pallas_call x1, Pallas kernels, per_device(): pl.pallas_call(functools.partial(kernel, sizes), out_shape=jax.ShapeDtype...  28.4 us
    reshape x1, local copies, waits for them, and re-layouts, per_device(): return out.reshape(T, 2 * R, 2 * C, MID)  1.74 us

profile of v1, /device:TPU:27, one launch (start us, length us, event | category | flops | bytes accessed | tf_op | source)
XLA Modules:
  0.0 30.1 jit_solution(2738766857905921548)
XLA Ops:
  0.0 28.4 %decoder_block.1 = bf16[4,8,16,256]{3,2,1,0:T(8,128)(2,1)} custom-call(bf16[4,4,16,256]{3,2,1,0:T(8,128)(2,1)} %latent.1, bf16[3,3,3,256,256]{4,3,2,1,0:T(8,128)(2,1)} %w1_hbm.1, bf16[3,3,3,256,128]{4,3,2,1,0:T(8,128)(2,1)} %w2_hbm.1, bf16[3,3,3,128,128]{4,3,2,1,0:T(8,128)(2,1)} %w3_hbm.1, bf16[2,400,224]{2,1,0:T(8,128)(2,1)} %constant.4.clone.sel_ref, ...), custom_call_target="tpu_custom_call" | custom-call | flops 7000000000 | bytes 8000000 | tf_op jit(solution)/shard_map/decoder_block/pallas_call | solution.py:418
  28.4 1.7 %reshape.3 = bf16[4,8,32,128]{3,2,1,0:T(8,128)(2,1)} reshape(bf16[4,8,16,256]{3,2,1,0:T(8,128)(2,1)} %decoder_block.1) | data formatting | bytes 524288 | tf_op jit(solution)/shard_map/reshape | solution.py:451

commit v2 on v1

--- a/solution.py
+++ b/solution.py
@@ -50,8 +50,8 @@
 
 
 def kernel(
-    sizes, latent, w1_hbm, w2_hbm, w3_hbm, sel_ref, pack_ref, out_ref,
-    rc, halo, pack, m0, m1, e9, f0, f1, e2, s0, s1, w1, w2, w2e, w3e,
+    sizes, latent, w1_hbm, w2_hbm, w3_hbm, sel_hbm, pack_ref, out_hbm,
+    rc, halo, pack, m0, m1, e9, f0, f1, e2, s0, s1, w1, w2, w2e, w3e, sel_ref, out_ref, woven,
     send, recv, ysend, yrecv, local,
 ):
     sections, rows, cols = sizes
@@ -125,6 +125,8 @@
 
     tile = pltpu.make_async_copy(latent, rc.at[6:10, 2:6], local.at[0])
     tile.start()
+    sel_copy = pltpu.make_async_copy(sel_hbm, sel_ref, local.at[11])
+    sel_copy.start()
     second_copy = pltpu.make_async_copy(w2_hbm, w2, local.at[1])
     second_copy.start()
     first_copy = pltpu.make_async_copy(w1_hbm, w1, local.at[2])
@@ -211,7 +213,7 @@
                         w2e[a, row : row + LAT, lane : lane + MID] = x.astype(BF16)
 
     def prepare(t):
-        g, t2 = t // 2, t % 2
+        g, t2 = t // 2, lax.rem(t, 2)
         rhs = jnp.concatenate(
             [rc[t].reshape(8 * C, LAT), halo[1, :, g].reshape(48, LAT), halo[0, :, g].reshape(48, LAT)],
             axis=0,
@@ -228,6 +230,11 @@
 
     def shifted_up(x, last):
         return jnp.where(row16 == 15, last, pltpu.roll(x, 15, 0))
+
+    def result(f):
+        return pltpu.make_async_copy(
+            out_ref.at[pl.ds(f, 2)], out_hbm.at[pl.ds(f, 2)], local.at[9 + f // 2]
+        )
 
     def conv1(f):
         shifts = (m0, m1, rc)
@@ -322,70 +329,84 @@
                             parts.append(x.reshape(64, 256))
                     blocks.append(jnp.concatenate(parts, axis=0))
         lhs = jnp.concatenate(blocks, axis=1)
-        total = jnp.dot(lhs, w3e[...].reshape(18 * 256, 256), preferred_element_type=F32).astype(BF16)
+        total = jnp.dot(lhs, w3e[...].reshape(18 * 256, 256), preferred_element_type=F32)
         for parity in range(2):
             for i in range(2):
                 for q in range(4):
                     at = parity * 128 + i * 64 + q * 16
-                    out_ref[f + i, 2 * q + parity] = total[at : at + 16]
-
+                    for fc in range(2):
+                        woven[fc::2] = total[at : at + 16, fc * MID : (fc + 1) * MID]
+                    out_ref[f + i, 2 * q + parity] = woven[...].astype(BF16)
+
+    sel_copy.wait()
     spatial_wait_recv("A")
-    for t in (8, 9, 6, 7):
+
+    @pl.loop(8, 10)
+    def _(t):
         prepare(t)
 
-    @pl.when(s > 0)
-    def _():
-        onward(0).wait_recv()
-
-        @pl.when(s < sections - 1)
-        def _():
-            onward(2).start()
-
-        make_pack(2)
-        spatial_start("B1")
-
-    first_copy.wait()
-    conv1(6)
-
-    @pl.when(s > 0)
-    def _():
-        onward(1).wait_recv()
-        make_pack(1)
-        spatial_start("B0")
-        spatial_wait_recv("B1")
-
-    prepare(4)
-    prepare(5)
-    conv1(4)
-    conv2(4)
-
-    @pl.when(s > 1)
-    def _():
-        onward(2).wait_recv()
-        make_pack(0)
-        spatial_start("C")
-
-    @pl.when(s > 0)
-    def _():
-        spatial_wait_recv("B0")
-
-    prepare(2)
-    prepare(3)
-    conv1(2)
-    conv2(2)
-    for copy in third_copies:
-        copy.wait()
-    conv3(2)
-
-    @pl.when(s > 1)
-    def _():
-        spatial_wait_recv("C")
-
-    prepare(0)
-    prepare(1)
-    conv1(0)
-    conv2(0)
-    conv3(0)
+    @pl.loop(0, 4)
+    def _(i):
+        f = 6 - 2 * i
+
+        @pl.when(jnp.logical_and(i == 0, s > 0))
+        def _():
+            onward(0).wait_recv()
+
+            @pl.when(s < sections - 1)
+            def _():
+                onward(2).start()
+
+            make_pack(2)
+            spatial_start("B1")
+
+        @pl.when(jnp.logical_and(i == 1, s > 0))
+        def _():
+            onward(1).wait_recv()
+            make_pack(1)
+            spatial_start("B0")
+            spatial_wait_recv("B1")
+
+        @pl.when(jnp.logical_and(i == 2, s > 1))
+        def _():
+            onward(2).wait_recv()
+            make_pack(0)
+            spatial_start("C")
+
+        @pl.when(jnp.logical_and(i == 2, s > 0))
+        def _():
+            spatial_wait_recv("B0")
+
+        @pl.when(jnp.logical_and(i == 3, s > 1))
+        def _():
+            spatial_wait_recv("C")
+
+        @pl.loop(0, 2)
+        def _(k):
+            prepare(f + k)
+
+        @pl.when(i == 0)
+        def _():
+            first_copy.wait()
+
+        conv1(f)
+
+        @pl.when(i >= 1)
+        def _():
+            conv2(f)
+
+        @pl.when(i == 2)
+        def _():
+            for copy in third_copies:
+                copy.wait()
+
+        @pl.when(i >= 2)
+        def _():
+            conv3(f)
+            result(f).start()
+
+    result(2).wait()
+    result(0).wait()
 
     spatial_wait_send("A")
 
@@ -417,9 +438,9 @@
         vmem = pl.BlockSpec(memory_space=pltpu.VMEM)
         out = pl.pallas_call(
             functools.partial(kernel, sizes),
-            out_shape=jax.ShapeDtypeStruct((T, 2 * R, C, 2 * MID), BF16),
-            in_specs=[hbm] * 4 + [vmem] * 2,
-            out_specs=vmem,
+            out_shape=jax.ShapeDtypeStruct((T, 2 * R, 2 * C, MID), BF16),
+            in_specs=[hbm] * 5 + [vmem],
+            out_specs=hbm,
             scratch_shapes=[
                 pltpu.VMEM((10, 8, C, LAT), BF16),
                 pltpu.VMEM((2, 3, 5, 16, LAT), BF16),
@@ -436,11 +457,14 @@
                 pltpu.VMEM((3, 3, 3, LAT, MID), BF16),
                 pltpu.VMEM((3, 4 * LAT, 4 * MID), BF16),
                 pltpu.VMEM((3, 2, 3, 2 * MID, 2 * MID), BF16),
+                pltpu.VMEM((2, 400, 224), BF16),
+                pltpu.VMEM((T, 2 * R, 2 * C, MID), BF16),
+                pltpu.VMEM((2 * C, MID), F32),
                 pltpu.SemaphoreType.DMA((4, 8)),
                 pltpu.SemaphoreType.DMA((4, 8)),
                 pltpu.SemaphoreType.DMA((3,)),
                 pltpu.SemaphoreType.DMA((3,)),
-                pltpu.SemaphoreType.DMA((9,)),
+                pltpu.SemaphoreType.DMA((12,)),
             ],
             compiler_params=pltpu.CompilerParams(
                 collective_id=0, has_side_effects=True, vmem_limit_bytes=56 * 1024 * 1024
@@ -448,7 +472,7 @@
             cost_estimate=pl.CostEstimate(flops=7 * 10**9, bytes_accessed=8 * 10**6, transcendentals=0),
             name="decoder_block",
         )(latent, w_first, w_second, w_third, jnp.asarray(sel), jnp.asarray(pack))
-        return out.reshape(T, 2 * R, 2 * C, MID)
+        return out
 
     spec = P("section", "row", "col", None)
     return jax.shard_map(

time: 30.4 us -> 26.2 us (0.86)
  Pallas kernels: 28.4 us -> 24.2 us
    pallas_call x1, Pallas kernels: 28.4 us -> 24.2 us  [per_device(): pl.pallas_call(functools.partial(kernel, sizes), out_shape=jax.ShapeDtype...]
    reshape x1 -> x0, local copies, waits for them, and re-layouts: 1.74 us -> none  [per_device(): return out.reshape(T, 2 * R, 2 * C, MID)]
    unnamed x0 -> x1, local copies, waits for them, and re-layouts: none -> 1.67 us
where the time goes in v2:
time: 26.2 us; the launch traced here: 25.9 us
  Pallas kernels  24.2 us (92%)
  local copies, waits for them, and re-layouts  1.67 us (6%)
    pallas_call x1, Pallas kernels, per_device(): pl.pallas_call(functools.partial(kernel, sizes), out_shape=jax.ShapeDtype...  24.2 us
    unnamed x1, local copies, waits for them, and re-layouts  1.67 us

profile of v2, /device:TPU:27, one launch (start us, length us, event | category | flops | bytes accessed | tf_op | source)
XLA Modules:
  0.0 25.9 jit_solution(6826569234863095721)
XLA Ops:
  0.0 24.2 %decoder_block.1 = bf16[4,8,32,128]{3,2,1,0:T(8,128)(2,1)} custom-call(bf16[4,4,16,256]{3,2,1,0:T(8,128)(2,1)} %latent.1, bf16[3,3,3,256,256]{4,3,2,1,0:T(8,128)(2,1)} %w1_hbm.1, bf16[3,3,3,256,128]{4,3,2,1,0:T(8,128)(2,1)} %w2_hbm.1, bf16[3,3,3,128,128]{4,3,2,1,0:T(8,128)(2,1)} %w3_hbm.1, bf16[2,400,224]{2,1,0:T(8,128)(2,1)} %constant.4.clone.sel_hbm, ...), custom_call_target="tpu_custom_call" | custom-call | flops 7000000000 | bytes 8000000 | tf_op jit(solution)/shard_map/decoder_block/pallas_call | solution.py:439
  24.2 1.7 %copy.8 = bf16[4,8,32,128]{3,2,1,0:T(8,128)(2,1)} copy(bf16[4,8,32,128]{3,2,1,0:T(8,128)(2,1)} %decoder_block.1) | data formatting | bytes 524288

commit v3 on v2

--- a/solution.py
+++ b/solution.py
@@ -14,32 +14,26 @@
 
 T, R, C = 4, 4, 16
 LAT, MID = 256, 128
-DIRS = [(dr, dc) for dr in (-1, 0, 1) for dc in (-1, 0, 1) if (dr, dc) != (0, 0)]
+DIRS = [(-1, 0), (1, 0), (-1, -1), (-1, 1), (1, -1), (1, 1), (0, -1), (0, 1)]
 GROUPS = {"A": (3, 5), "B1": (2, 3), "B0": (1, 2), "C": (0, 1)}
 ORDER = {"A": 0, "B1": 1, "B0": 2, "C": 3}
 TAPS = [(dr, dc) for dr in range(3) for dc in range(3)]
 
 
 def selections():
-    sel = np.zeros((2, 400, 224), np.float32)
+    sel = np.zeros((2, 144, 176), np.float32)
 
     def source(t2, row, col):
-        if 2 <= col < 18:
+        if col < 18:
             return row * C + col - 2
-        side = 0 if col < 2 else 1
         slot, r = (0, row + 2) if row < 2 else (1, row - 2) if row < 6 else (2, row - 6)
-        base = 128 if side == 1 else 176
-        return base + slot * 16 + r * 4 + t2 * 2 + (col if side == 0 else col - 18)
+        return 128 + slot * 16 + r * 4 + t2 * 2 + col - 18
 
     for t2 in range(2):
-        for row in range(8):
-            for j in range(C):
-                sel[t2, row * C + j, source(t2, row, j)] = 1
-                sel[t2, 128 + row * C + j, source(t2, row, j + 1)] = 1
         for tap, (dr, dc) in enumerate(TAPS):
             for j in range(2):
                 for r in range(6):
-                    sel[t2, 256 + tap * 16 + j * 8 + r, source(t2, r + dr, 16 + j + dc)] = 1
+                    sel[t2, tap * 16 + j * 8 + r, source(t2, r + dr, 16 + j + dc)] = 1
     pack = np.zeros((32, 128), np.float32)
     for side in range(2):
         for r in range(R):
@@ -50,8 +44,8 @@
 
 
 def kernel(
-    sizes, latent, w1_hbm, w2_hbm, w3_hbm, sel_hbm, pack_ref, out_hbm,
-    rc, halo, pack, m0, m1, e9, f0, f1, e2, s0, s1, w1, w2, w2e, w3e, sel_ref, out_ref, woven,
+    sizes, latent, w1_hbm, w2_hbm, w3_hbm, sel_hbm, pick_hbm, out_ref,
+    rc, halo, pack, m0, m1, e9, f0, f1, e2, s0, s1, w1, w2, w2e, w3e, sel_ref, pick_ref, woven,
     send, recv, ysend, yrecv, local,
 ):
     sections, rows, cols = sizes
@@ -93,6 +87,9 @@
 
     def spatial_start(group):
         for k in range(8):
+            if k == 2 and group != "A":
+                make_pack(GROUPS[group][0])
+
             @pl.when(sends(k))
             def _():
                 spatial(group, k).start()
@@ -119,14 +116,21 @@
 
     def make_pack(g):
         own = rc[2 * g : 2 * g + 2, 2:6].reshape(2 * R * C, LAT)
-        both = jnp.dot(pack_ref[...], own, preferred_element_type=F32).astype(BF16)
+        both = jnp.dot(pick_ref[...], own, preferred_element_type=F32).astype(BF16)
         pack[0, g] = both[0:16]
         pack[1, g] = both[16:32]
 
+    barrier = pltpu.get_barrier_semaphore()
+    partners = [(-1, 0, 0)] + [(0, dr, dc) for dr, dc in reversed(DIRS)] + [(1, 0, 0)]
+    for d in partners:
+        pl.semaphore_signal(barrier, inc=1, device_id=device(*d), device_id_type=MESH)
+
     tile = pltpu.make_async_copy(latent, rc.at[6:10, 2:6], local.at[0])
     tile.start()
-    sel_copy = pltpu.make_async_copy(sel_hbm, sel_ref, local.at[11])
+    sel_copy = pltpu.make_async_copy(sel_hbm, sel_ref, local.at[10])
     sel_copy.start()
+    pick_copy = pltpu.make_async_copy(pick_hbm, pick_ref, local.at[9])
+    pick_copy.start()
     second_copy = pltpu.make_async_copy(w2_hbm, w2, local.at[1])
     second_copy.start()
     first_copy = pltpu.make_async_copy(w1_hbm, w1, local.at[2])
@@ -143,12 +147,8 @@
         copy.start()
         third_copies.append(copy)
 
-    barrier = pltpu.get_barrier_semaphore()
-    partners = [(0, dr, dc) for dr, dc in DIRS] + [(1, 0, 0), (-1, 0, 0)]
-    for d in partners:
-        pl.semaphore_signal(barrier, inc=1, device_id=device(*d), device_id_type=MESH)
-
     tile.wait()
+    pick_copy.wait()
     make_pack(4)
     make_pack(3)
     pl.semaphore_wait(barrier, len(partners))
@@ -212,17 +212,22 @@
                         row = (q * 2 + p) * LAT
                         w2e[a, row : row + LAT, lane : lane + MID] = x.astype(BF16)
 
-    def prepare(t):
-        g, t2 = t // 2, lax.rem(t, 2)
-        rhs = jnp.concatenate(
-            [rc[t].reshape(8 * C, LAT), halo[1, :, g].reshape(48, LAT), halo[0, :, g].reshape(48, LAT)],
-            axis=0,
-        )
-        moved = jnp.dot(sel_ref[t2], rhs, preferred_element_type=F32).astype(BF16)
-        m0[t] = moved[0:128].reshape(8, C, LAT)
-        m1[t] = moved[128:256].reshape(8, C, LAT)
-        for tap in range(9):
-            e9[t, :, tap * LAT : (tap + 1) * LAT] = moved[256 + tap * 16 : 272 + tap * 16]
+    def prepare(g):
+        left = [halo[0, slot, g].astype(F32) for slot in range(3)]
+        for t2 in range(2):
+            t = 2 * g + t2
+            rhs = jnp.concatenate([rc[t].reshape(8 * C, LAT), halo[1, :, g].reshape(48, LAT)], axis=0)
+            moved = jnp.dot(sel_ref[t2], rhs, preferred_element_type=F32).astype(BF16)
+            for tap in range(9):
+                e9[t, :, tap * LAT : (tap + 1) * LAT] = moved[tap * 16 : tap * 16 + 16]
+            for row in range(8):
+                slot, k = (0, row + 2) if row < 2 else (1, row - 2) if row < 6 else (2, row - 6)
+                k = k * 4 + t2 * 2
+                x = pltpu.roll(rc[t, row].astype(F32), 1, 0)
+                x = jnp.where(row16 == 0, left[slot][k + 1 : k + 2], x)
+                m1[t, row] = x.astype(BF16)
+                x = jnp.where(row16 == 0, left[slot][k : k + 1], pltpu.roll(x, 1, 0))
+                m0[t, row] = x.astype(BF16)
 
     row16 = lax.broadcasted_iota(jnp.int32, (16, 1), 0)
     top, bottom = r == 0, r == rows - 1
@@ -230,11 +235,6 @@
 
     def shifted_up(x, last):
         return jnp.where(row16 == 15, last, pltpu.roll(x, 15, 0))
-
-    def result(f):
-        return pltpu.make_async_copy(
-            out_ref.at[pl.ds(f, 2)], out_hbm.at[pl.ds(f, 2)], local.at[9 + f // 2]
-        )
 
     def conv1(f):
         shifts = (m0, m1, rc)
@@ -338,39 +338,32 @@
                         woven[fc::2] = total[at : at + 16, fc * MID : (fc + 1) * MID]
                     out_ref[f + i, 2 * q + parity] = woven[...].astype(BF16)
 
+    @pl.when(s > 0)
+    def _():
+        onward(0).wait_recv()
+
+        @pl.when(s < sections - 1)
+        def _():
+            onward(2).start()
+
+        spatial_start("B1")
+
     sel_copy.wait()
     spatial_wait_recv("A")
-
-    @pl.loop(8, 10)
-    def _(t):
-        prepare(t)
 
     @pl.loop(0, 4)
     def _(i):
         f = 6 - 2 * i
 
-        @pl.when(jnp.logical_and(i == 0, s > 0))
-        def _():
-            onward(0).wait_recv()
-
-            @pl.when(s < sections - 1)
-            def _():
-                onward(2).start()
-
-            make_pack(2)
-            spatial_start("B1")
-
         @pl.when(jnp.logical_and(i == 1, s > 0))
         def _():
             onward(1).wait_recv()
-            make_pack(1)
             spatial_start("B0")
             spatial_wait_recv("B1")
 
         @pl.when(jnp.logical_and(i == 2, s > 1))
         def _():
             onward(2).wait_recv()
-            make_pack(0)
             spatial_start("C")
 
         @pl.when(jnp.logical_and(i == 2, s > 0))
@@ -381,9 +374,9 @@
         def _():
             spatial_wait_recv("C")
 
-        @pl.loop(0, 2)
+        @pl.loop(jnp.where(i == 0, 0, 1), 2)
         def _(k):
-            prepare(f + k)
+            prepare(4 - i - k)
 
         @pl.when(i == 0)
         def _():
@@ -403,10 +396,7 @@
         @pl.when(i >= 2)
         def _():
             conv3(f)
-            result(f).start()
-
-    result(2).wait()
-    result(0).wait()
+
 
     spatial_wait_send("A")
 
@@ -438,9 +428,9 @@
         vmem = pl.BlockSpec(memory_space=pltpu.VMEM)
         out = pl.pallas_call(
             functools.partial(kernel, sizes),
-            out_shape=jax.ShapeDtypeStruct((T, 2 * R, 2 * C, MID), BF16),
-            in_specs=[hbm] * 5 + [vmem],
-            out_specs=hbm,
+            out_shape=pltpu.VMEM((T, 2 * R, 2 * C, MID), BF16),
+            in_specs=[hbm] * 6,
+            out_specs=vmem,
             scratch_shapes=[
                 pltpu.VMEM((10, 8, C, LAT), BF16),
                 pltpu.VMEM((2, 3, 5, 16, LAT), BF16),
@@ -457,14 +447,14 @@
                 pltpu.VMEM((3, 3, 3, LAT, MID), BF16),
                 pltpu.VMEM((3, 4 * LAT, 4 * MID), BF16),
                 pltpu.VMEM((3, 2, 3, 2 * MID, 2 * MID), BF16),
-                pltpu.VMEM((2, 400, 224), BF16),
-                pltpu.VMEM((T, 2 * R, 2 * C, MID), BF16),
+                pltpu.VMEM((2, 144, 176), BF16),
+                pltpu.VMEM((32, 2 * R * C), BF16),
                 pltpu.VMEM((2 * C, MID), F32),
                 pltpu.SemaphoreType.DMA((4, 8)),
                 pltpu.SemaphoreType.DMA((4, 8)),
                 pltpu.SemaphoreType.DMA((3,)),
                 pltpu.SemaphoreType.DMA((3,)),
-                pltpu.SemaphoreType.DMA((12,)),
+                pltpu.SemaphoreType.DMA((11,)),
             ],
             compiler_params=pltpu.CompilerParams(
                 collective_id=0, has_side_effects=True, vmem_limit_bytes=56 * 1024 * 1024

time: 26.2 us -> 23.1 us (0.88)
  the two profiles are of different devices: /device:TPU:27 before, /device:TPU:24 now
where the time goes in v3:
time: 23.1 us; the launch traced here: 23 us
  Pallas kernels  22.3 us (97%)
  local copies, waits for them, and re-layouts  0.71 us (3%)
    pallas_call x1, Pallas kernels, per_device(): pl.pallas_call(functools.partial(kernel, sizes), out_shape=pltpu.VMEM((T,...  22.3 us
    unnamed x1, local copies, waits for them, and re-layouts  0.71 us

profile of v3, /device:TPU:24, one launch (start us, length us, event | category | flops | bytes accessed | tf_op | source)
XLA Modules:
  0.0 23.0 jit_solution(18244802118401237524)
XLA Ops:
  0.0 22.3 %decoder_block.1 = bf16[4,8,32,128]{3,2,1,0:T(8,128)(2,1)S(1)} custom-call(bf16[4,4,16,256]{3,2,1,0:T(8,128)(2,1)} %latent.1, bf16[3,3,3,256,256]{4,3,2,1,0:T(8,128)(2,1)} %w1_hbm.1, bf16[3,3,3,256,128]{4,3,2,1,0:T(8,128)(2,1)} %w2_hbm.1, bf16[3,3,3,128,128]{4,3,2,1,0:T(8,128)(2,1)} %w3_hbm.1, bf16[2,144,176]{2,1,0:T(8,128)(2,1)} %constant.4.clone.sel_hbm, ...), custom_call_target="tpu_custom_call" | custom-call | flops 7000000000 | bytes 8000000 | tf_op jit(solution)/shard_map/decoder_block/pallas_call | solution.py:429
  22.3 0.7 %copy.8 = bf16[4,8,32,128]{3,2,1,0:T(8,128)(2,1)} copy(bf16[4,8,32,128]{3,2,1,0:T(8,128)(2,1)S(1)} %decoder_block.1) | data formatting | bytes 524288

commit v4 on v3

--- a/solution.py
+++ b/solution.py
@@ -121,7 +121,7 @@
         pack[1, g] = both[16:32]
 
     barrier = pltpu.get_barrier_semaphore()
-    partners = [(-1, 0, 0)] + [(0, dr, dc) for dr, dc in reversed(DIRS)] + [(1, 0, 0)]
+    partners = [(-1, 0, 0)] + [(0, dr, dc) for dr, dc in DIRS] + [(1, 0, 0)]
     for d in partners:
         pl.semaphore_signal(barrier, inc=1, device_id=device(*d), device_id_type=MESH)
 
@@ -361,11 +361,6 @@
             spatial_start("B0")
             spatial_wait_recv("B1")
 
-        @pl.when(jnp.logical_and(i == 2, s > 1))
-        def _():
-            onward(2).wait_recv()
-            spatial_start("C")
-
         @pl.when(jnp.logical_and(i == 2, s > 0))
         def _():
             spatial_wait_recv("B0")
@@ -383,6 +378,11 @@
             first_copy.wait()
 
         conv1(f)
+
+        @pl.when(jnp.logical_and(i == 1, s > 1))
+        def _():
+            onward(2).wait_recv()
+            spatial_start("C")
 
         @pl.when(i >= 1)
         def _():

time: 23.1 us -> 22.4 us (0.970)
  the two profiles are of different devices: /device:TPU:24 before, /device:TPU:27 now
where the time goes in v4:
time: 22.4 us; the launch traced here: 22.3 us
  Pallas kernels  21.6 us (96%)
  local copies, waits for them, and re-layouts  0.71 us (3%)
    pallas_call x1, Pallas kernels, per_device(): pl.pallas_call(functools.partial(kernel, sizes), out_shape=pltpu.VMEM((T,...  21.6 us
    unnamed x1, local copies, waits for them, and re-layouts  0.71 us

profile of v4, /device:TPU:27, one launch (start us, length us, event | category | flops | bytes accessed | tf_op | source)
XLA Modules:
  0.0 22.3 jit_solution(13412430716197027788)
XLA Ops:
  0.0 21.6 %decoder_block.1 = bf16[4,8,32,128]{3,2,1,0:T(8,128)(2,1)S(1)} custom-call(bf16[4,4,16,256]{3,2,1,0:T(8,128)(2,1)} %latent.1, bf16[3,3,3,256,256]{4,3,2,1,0:T(8,128)(2,1)} %w1_hbm.1, bf16[3,3,3,256,128]{4,3,2,1,0:T(8,128)(2,1)} %w2_hbm.1, bf16[3,3,3,128,128]{4,3,2,1,0:T(8,128)(2,1)} %w3_hbm.1, bf16[2,144,176]{2,1,0:T(8,128)(2,1)} %constant.4.clone.sel_hbm, ...), custom_call_target="tpu_custom_call" | custom-call | flops 7000000000 | bytes 8000000 | tf_op jit(solution)/shard_map/decoder_block/pallas_call | solution.py:429
  21.6 0.7 %copy.8 = bf16[4,8,32,128]{3,2,1,0:T(8,128)(2,1)} copy(bf16[4,8,32,128]{3,2,1,0:T(8,128)(2,1)S(1)} %decoder_block.1) | data formatting | bytes 524288

commit v5 on v4

--- a/solution.py
+++ b/solution.py
@@ -34,18 +34,12 @@
             for j in range(2):
                 for r in range(6):
                     sel[t2, tap * 16 + j * 8 + r, source(t2, r + dr, 16 + j + dc)] = 1
-    pack = np.zeros((32, 128), np.float32)
-    for side in range(2):
-        for r in range(R):
-            for t2 in range(2):
-                for c in range(2):
-                    pack[side * 16 + r * 4 + t2 * 2 + c, t2 * 64 + r * C + c + 14 * side] = 1
-    return sel.astype(jnp.bfloat16), pack.astype(jnp.bfloat16)
+    return sel.astype(jnp.bfloat16)
 
 
 def kernel(
-    sizes, latent, w1_hbm, w2_hbm, w3_hbm, sel_hbm, pick_hbm, out_ref,
-    rc, halo, pack, m0, m1, e9, f0, f1, e2, s0, s1, w1, w2, w2e, w3e, sel_ref, pick_ref, woven,
+    sizes, latent, w1_hbm, w2_hbm, w3_hbm, sel_hbm, out_ref,
+    rc, halo, pack, m0, m1, e9, f0, f1, e2, s0, s1, w1, w2, w2e, w3e, sel_ref, woven,
     send, recv, ysend, yrecv, local,
 ):
     sections, rows, cols = sizes
@@ -114,11 +108,22 @@
             device_id=device(1, 0, 0), device_id_type=MESH,
         )
 
+    row8 = lax.broadcasted_iota(jnp.int32, (8, 1), 0)
+
     def make_pack(g):
-        own = rc[2 * g : 2 * g + 2, 2:6].reshape(2 * R * C, LAT)
-        both = jnp.dot(pick_ref[...], own, preferred_element_type=F32).astype(BF16)
-        pack[0, g] = both[0:16]
-        pack[1, g] = both[16:32]
+        halves = [[jnp.zeros((8, LAT), F32)] * 2 for _ in range(2)]
+        for q in range(R):
+            for t2 in range(2):
+                half, at = divmod(q * 4 + t2 * 2, 8)
+                x = rc[2 * g + t2, 2 + q].astype(F32)
+                here = jnp.logical_and(row8 >= at, row8 < at + 2)
+                for side, y in ((0, x[0:8]), (1, x[8:16])):
+                    by = (at - 6 * side) % 8
+                    if by:
+                        y = pltpu.roll(y, by, 0)
+                    halves[side][half] = jnp.where(here, y, halves[side][half])
+        for side in range(2):
+            pack[side, g] = jnp.concatenate(halves[side], axis=0).astype(BF16)
 
     barrier = pltpu.get_barrier_semaphore()
     partners = [(-1, 0, 0)] + [(0, dr, dc) for dr, dc in DIRS] + [(1, 0, 0)]
@@ -127,10 +132,8 @@
 
     tile = pltpu.make_async_copy(latent, rc.at[6:10, 2:6], local.at[0])
     tile.start()
-    sel_copy = pltpu.make_async_copy(sel_hbm, sel_ref, local.at[10])
+    sel_copy = pltpu.make_async_copy(sel_hbm, sel_ref, local.at[9])
     sel_copy.start()
-    pick_copy = pltpu.make_async_copy(pick_hbm, pick_ref, local.at[9])
-    pick_copy.start()
     second_copy = pltpu.make_async_copy(w2_hbm, w2, local.at[1])
     second_copy.start()
     first_copy = pltpu.make_async_copy(w1_hbm, w1, local.at[2])
@@ -148,7 +151,6 @@
         third_copies.append(copy)
 
     tile.wait()
-    pick_copy.wait()
     make_pack(4)
     make_pack(3)
     pl.semaphore_wait(barrier, len(partners))
@@ -421,7 +423,7 @@
 
 def solution(mesh):
     sizes = tuple(mesh.shape[a] for a in ("section", "row", "col"))
-    sel, pack = selections()
+    sel = selections()
 
     def per_device(latent, w_first, w_second, w_third):
         hbm = pl.BlockSpec(memory_space=pltpu.HBM)
@@ -429,7 +431,7 @@
         out = pl.pallas_call(
             functools.partial(kernel, sizes),
             out_shape=pltpu.VMEM((T, 2 * R, 2 * C, MID), BF16),
-            in_specs=[hbm] * 6,
+            in_specs=[hbm] * 5,
             out_specs=vmem,
             scratch_shapes=[
                 pltpu.VMEM((10, 8, C, LAT), BF16),
@@ -448,20 +450,19 @@
                 pltpu.VMEM((3, 4 * LAT, 4 * MID), BF16),
                 pltpu.VMEM((3, 2, 3, 2 * MID, 2 * MID), BF16),
                 pltpu.VMEM((2, 144, 176), BF16),
-                pltpu.VMEM((32, 2 * R * C), BF16),
                 pltpu.VMEM((2 * C, MID), F32),
                 pltpu.SemaphoreType.DMA((4, 8)),
                 pltpu.SemaphoreType.DMA((4, 8)),
                 pltpu.SemaphoreType.DMA((3,)),
                 pltpu.SemaphoreType.DMA((3,)),
-                pltpu.SemaphoreType.DMA((11,)),
+                pltpu.SemaphoreType.DMA((10,)),
             ],
             compiler_params=pltpu.CompilerParams(
                 collective_id=0, has_side_effects=True, vmem_limit_bytes=56 * 1024 * 1024
             ),
             cost_estimate=pl.CostEstimate(flops=7 * 10**9, bytes_accessed=8 * 10**6, transcendentals=0),
             name="decoder_block",
-        )(latent, w_first, w_second, w_third, jnp.asarray(sel), jnp.asarray(pack))
+        )(latent, w_first, w_second, w_third, jnp.asarray(sel))
         return out
 
     spec = P("section", "row", "col", None)

time: 22.4 us -> 22.3 us (level)
  no operation moved by 1% of the time
where the time goes in v5:
time: 22.3 us; the launch traced here: 22.2 us
  Pallas kernels  21.5 us (96%)
  local copies, waits for them, and re-layouts  0.71 us (3%)
    pallas_call x1, Pallas kernels, per_device(): pl.pallas_call(functools.partial(kernel, sizes), out_shape=pltpu.VMEM((T,...  21.5 us
    unnamed x1, local copies, waits for them, and re-layouts  0.71 us

profile of v5, /device:TPU:27, one launch (start us, length us, event | category | flops | bytes accessed | tf_op | source)
XLA Modules:
  0.0 22.2 jit_solution(542154924986506519)
XLA Ops:
  0.0 21.5 %decoder_block.1 = bf16[4,8,32,128]{3,2,1,0:T(8,128)(2,1)S(1)} custom-call(bf16[4,4,16,256]{3,2,1,0:T(8,128)(2,1)} %latent.1, bf16[3,3,3,256,256]{4,3,2,1,0:T(8,128)(2,1)} %w1_hbm.1, bf16[3,3,3,256,128]{4,3,2,1,0:T(8,128)(2,1)} %w2_hbm.1, bf16[3,3,3,128,128]{4,3,2,1,0:T(8,128)(2,1)} %w3_hbm.1, bf16[2,144,176]{2,1,0:T(8,128)(2,1)} %constant.2.clone.sel_hbm), custom_call_target="tpu_custom_call" | custom-call | flops 7000000000 | bytes 8000000 | tf_op jit(solution)/shard_map/decoder_block/pallas_call | solution.py:431
  21.5 0.7 %copy.7 = bf16[4,8,32,128]{3,2,1,0:T(8,128)(2,1)} copy(bf16[4,8,32,128]{3,2,1,0:T(8,128)(2,1)S(1)} %decoder_block.1) | data formatting | bytes 524288

commit v6 on v5

--- a/solution.py
+++ b/solution.py
@@ -361,14 +361,36 @@
         def _():
             onward(1).wait_recv()
             spatial_start("B0")
+
+        @pl.when(i == 1)
+        def _():
+            spatial_wait_send("A")
+
+        @pl.when(jnp.logical_and(i == 1, s < sections - 1))
+        def _():
+            onward(0).wait_send()
+            onward(1).wait_send()
+
+        @pl.when(jnp.logical_and(i == 1, s > 0))
+        def _():
             spatial_wait_recv("B1")
 
         @pl.when(jnp.logical_and(i == 2, s > 0))
         def _():
             spatial_wait_recv("B0")
 
+        @pl.when(jnp.logical_and(i == 3, s > 0))
+        def _():
+            spatial_wait_send("B1")
+            spatial_wait_send("B0")
+
+            @pl.when(s < sections - 1)
+            def _():
+                onward(2).wait_send()
+
         @pl.when(jnp.logical_and(i == 3, s > 1))
         def _():
+            spatial_wait_send("C")
             spatial_wait_recv("C")
 
         @pl.loop(jnp.where(i == 0, 0, 1), 2)
@@ -398,27 +420,6 @@
         @pl.when(i >= 2)
         def _():
             conv3(f)
-
-
-    spatial_wait_send("A")
-
-    @pl.when(s < sections - 1)
-    def _():
-        onward(0).wait_send()
-        onward(1).wait_send()
-
-    @pl.when(s > 0)
-    def _():
-        spatial_wait_send("B1")
-        spatial_wait_send("B0")
-
-        @pl.when(s < sections - 1)
-        def _():
-            onward(2).wait_send()
-
-    @pl.when(s > 1)
-    def _():
-        spatial_wait_send("C")
 
 
 def solution(mesh):

time: 22.3 us -> 22.6 us (1.013)
  Pallas kernels: 21.5 us -> 21.9 us
    pallas_call x1, Pallas kernels: 21.5 us -> 21.9 us  [per_device(): pl.pallas_call(functools.partial(kernel, sizes), out_shape=pltpu.VMEM((T,...]
where the time goes in v6:
time: 22.6 us
  Pallas kernels  21.9 us (97%)
  local copies, waits for them, and re-layouts  0.71 us (3%)
    pallas_call x1, Pallas kernels, per_device(): pl.pallas_call(functools.partial(kernel, sizes), out_shape=pltpu.VMEM((T,...  21.9 us
    unnamed x1, local copies, waits for them, and re-layouts  0.71 us

profile of v6, /device:TPU:27, one launch (start us, length us, event | category | flops | bytes accessed | tf_op | source)
XLA Modules:
  0.0 22.6 jit_solution(2142341632570853170)
XLA Ops:
  0.0 21.9 %decoder_block.1 = bf16[4,8,32,128]{3,2,1,0:T(8,128)(2,1)S(1)} custom-call(bf16[4,4,16,256]{3,2,1,0:T(8,128)(2,1)} %latent.1, bf16[3,3,3,256,256]{4,3,2,1,0:T(8,128)(2,1)} %w1_hbm.1, bf16[3,3,3,256,128]{4,3,2,1,0:T(8,128)(2,1)} %w2_hbm.1, bf16[3,3,3,128,128]{4,3,2,1,0:T(8,128)(2,1)} %w3_hbm.1, bf16[2,144,176]{2,1,0:T(8,128)(2,1)} %constant.2.clone.sel_hbm), custom_call_target="tpu_custom_call" | custom-call | flops 7000000000 | bytes 8000000 | tf_op jit(solution)/shard_map/decoder_block/pallas_call | solution.py:432
  21.9 0.7 %copy.7 = bf16[4,8,32,128]{3,2,1,0:T(8,128)(2,1)} copy(bf16[4,8,32,128]{3,2,1,0:T(8,128)(2,1)S(1)} %decoder_block.1) | data formatting | bytes 524288

commit v7 on v5

--- a/solution.py
+++ b/solution.py
@@ -79,26 +79,34 @@
         dr, dc = DIRS[k]
         return jnp.logical_and(inside(r - dr, rows), inside(c - dc, cols))
 
+    interior = jnp.logical_and(
+        jnp.logical_and(r > 0, r < rows - 1), jnp.logical_and(c > 0, c < cols - 1)
+    )
+
+    def each(ks, condition, action):
+        @pl.when(interior)
+        def _():
+            for k in ks:
+                action(k)
+
+        @pl.when(jnp.logical_not(interior))
+        def _():
+            for k in ks:
+                @pl.when(condition(k))
+                def _():
+                    action(k)
+
     def spatial_start(group):
-        for k in range(8):
-            if k == 2 and group != "A":
-                make_pack(GROUPS[group][0])
-
-            @pl.when(sends(k))
-            def _():
-                spatial(group, k).start()
+        each(range(2), sends, lambda k: spatial(group, k).start())
+        if group != "A":
+            make_pack(GROUPS[group][0])
+        each(range(2, 8), sends, lambda k: spatial(group, k).start())
 
     def spatial_wait_recv(group):
-        for k in range(8):
-            @pl.when(receives(k))
-            def _():
-                spatial(group, k).wait_recv()
+        each(range(8), receives, lambda k: spatial(group, k).wait_recv())
 
     def spatial_wait_send(group):
-        for k in range(8):
-            @pl.when(sends(k))
-            def _():
-                spatial(group, k).wait_send()
+        each(range(8), sends, lambda k: spatial(group, k).wait_send())
 
     def onward(n):
         src, dst = ((8, 4), (6, 2), (4, 0))[n]

time: 22.3 us -> 22.5 us (level)
  no operation moved by 1% of the time
where the time goes in v7:
time: 22.5 us; the launch traced here: 22.4 us
  Pallas kernels  21.7 us (96%)
  local copies, waits for them, and re-layouts  0.71 us (3%)
    pallas_call x1, Pallas kernels, per_device(): pl.pallas_call(functools.partial(kernel, sizes), out_shape=pltpu.VMEM((T,...  21.7 us
    unnamed x1, local copies, waits for them, and re-layouts  0.71 us

profile of v7, /device:TPU:27, one launch (start us, length us, event | category | flops | bytes accessed | tf_op | source)
XLA Modules:
  0.0 22.4 jit_solution(7818106955275898631)
XLA Ops:
  0.0 21.7 %decoder_block.1 = bf16[4,8,32,128]{3,2,1,0:T(8,128)(2,1)S(1)} custom-call(bf16[4,4,16,256]{3,2,1,0:T(8,128)(2,1)} %latent.1, bf16[3,3,3,256,256]{4,3,2,1,0:T(8,128)(2,1)} %w1_hbm.1, bf16[3,3,3,256,128]{4,3,2,1,0:T(8,128)(2,1)} %w2_hbm.1, bf16[3,3,3,128,128]{4,3,2,1,0:T(8,128)(2,1)} %w3_hbm.1, bf16[2,144,176]{2,1,0:T(8,128)(2,1)} %constant.2.clone.sel_hbm), custom_call_target="tpu_custom_call" | custom-call | flops 7000000000 | bytes 8000000 | tf_op jit(solution)/shard_map/decoder_block/pallas_call | solution.py:439
  21.7 0.7 %copy.7 = bf16[4,8,32,128]{3,2,1,0:T(8,128)(2,1)} copy(bf16[4,8,32,128]{3,2,1,0:T(8,128)(2,1)S(1)} %decoder_block.1) | data formatting | bytes 524288
